TPU v7x, 512 devices: a whole 4x4x16 slice. The times are simulated.
512 devices in a mesh: row: 16 (over z_lo, core), col: 32 (over x, z_hi, y).
Axes of the slice: x: 4, y: 4, z: 16 (z_hi: 2, z_lo: 8; z = z_hi * 8 + z_lo), core: 2. Of those that a mesh axis runs over, the one named last changes fastest.
Arguments:
- embeddings: bfloat16 [393216, 1024], P(('row', 'col')), may hold values from -40 to 40
- doc_ids: int32 [393216], P(('row', 'col')), may hold values from 0 to 393215, each once
- valid_counts: int32 [512], P(('row', 'col')), may hold values from 384 to 768
Outputs:
- nearest: float32 [393216], P(('row', 'col'))
Inputs may be any that keep to these rules, and one draw needn't show every extreme that they name: `doc_ids`: the ids are distinct.
All inputs are finite; a program needn't handle non-finite values.
Results may differ from a plain program's by a relative error of at most 0.0005.
Values may be sent and summed in bfloat16 or wider, within the bound.
A program may use at most 64 MiB of HBM per device.

v0:
```python
import jax
import jax.numpy as jnp
from jax import lax
from jax.sharding import PartitionSpec as P

BAND = 4


def passed_along(array, axis, by):
    devices = lax.axis_size(axis)
    pairs = [(i, i + by) for i in range(devices) if 0 <= i + by < devices]
    return lax.ppermute(array, axis, pairs)


def passed_along_2(block, axis, distance):
    devices = range(lax.axis_size(axis))
    route = [((i - distance) % len(devices), i) for i in devices]
    return lax.ppermute(block, axis, route)


def normalize(embeddings):
    floats = embeddings.astype(jnp.float32)
    total = jnp.sum(floats * floats, axis=-1, keepdims=True)
    return (floats * lax.rsqrt(total + 1e-06)).astype(jnp.bfloat16)


def pair_maxima(unit_left, ids_left, valid_left, unit_right, ids_right, valid_right):
    scores = lax.dot_general(
        unit_left, unit_right, (((1,), (1,)), ((), ())), preferred_element_type=jnp.float32
    )
    both = valid_left[:, None] & valid_right[None, :]
    lower = both & (ids_right[None, :] < ids_left[:, None])
    upper = both & (ids_left[:, None] < ids_right[None, :])
    row_best = jnp.max(jnp.where(lower, scores, -1.0), axis=1)
    col_best = jnp.max(jnp.where(upper, scores, -1.0), axis=0)
    return (row_best, col_best)


def local(embeddings, doc_ids, valid_counts):
    row_count = embeddings.shape[0]
    unit_own = normalize(embeddings)
    positions = lax.iota(jnp.int32, row_count)
    valid_own = positions < valid_counts[0]
    nearest, unused = pair_maxima(unit_own, doc_ids, valid_own, unit_own, doc_ids, valid_own)
    col_list = []
    for shift_by in range(1, BAND + 1):
        partner = passed_along((unit_own, doc_ids, valid_counts), ("row", "col"), -shift_by)
        unit_other, ids_other, count_other = partner
        valid_other = positions < count_other[0]
        row_best, col_best = pair_maxima(
            unit_own, doc_ids, valid_own, unit_other, ids_other, valid_other
        )
        nearest = jnp.maximum(nearest, row_best)
        col_list.append(col_best)
    for shift_by in range(1, BAND + 1):
        returned = passed_along_2(col_list[shift_by - 1], ("row", "col"), shift_by)
        nearest = jnp.maximum(nearest, returned)
    return nearest


def solution(mesh):
    in_specs = (P(("row", "col"), None), P(("row", "col")), P(("row", "col")))
    out_specs = P(("row", "col"))
    return jax.shard_map(local, mesh=mesh, in_specs=in_specs, out_specs=out_specs, check_vma=False)
```

profile of v0, /device:TPU:224, one launch (start us, length us, event | category | flops | bytes accessed | tf_op | source)
XLA Modules:
  0.0 877.3 jit_solution(5387253137653851625)
XLA Ops:
  0.0 1.9 fusion
  2.3 10.4 %collective-permute-start.8 = (bf16[768,1024]{1,0:T(8,128)(2,1)S(1)}, bf16[768,1024]{1,0:T(8,128)(2,1)S(1)}, u32[]{:S(2)}, u32[]{:S(2)}) collective-permute-start(bf16[768,1024]{1,0:T(8,128)(2,1)S(1)} %fusion.1), channel_id=1, source_target_pairs={{3,0},{4,1},{5,2},{6,3},{7,4},{8,5},{9,6},{10,7},{11,8},{12,9},{13... | collective-permute-start | bytes 4718600 | tf_op jit(solution)/shard_map/ppermute | solution.py:12
  12.7 5.2 collective-permute-start.11
  17.9 11.4 %collective-permute-start.5 = (bf16[768,1024]{1,0:T(8,128)(2,1)S(1)}, bf16[768,1024]{1,0:T(8,128)(2,1)S(1)}, u32[]{:S(2)}, u32[]{:S(2)}) collective-permute-start(bf16[768,1024]{1,0:T(8,128)(2,1)S(1)} %fusion.1), channel_id=1, source_target_pairs={{2,0},{3,1},{4,2},{5,3},{6,4},{7,5},{8,6},{9,7},{10,8},{11,9},{12,... | collective-permute-start | bytes 4718600 | tf_op jit(solution)/shard_map/ppermute | solution.py:12
  29.3 3.0 collective-permute-start.2
  32.3 5.2 collective-permute-start.9
  38.1 719.5 %collective-permute-done.9 = s32[1]{0:T(128)} collective-permute-done((s32[1]{0:T(128)}, s32[1]{0:T(128)}, u32[]{:S(2)}, u32[]{:S(2)}) %collective-permute-start.9) | collective-permute-done | bytes 36 | tf_op jit(solution)/shard_map/ppermute | solution.py:12
  757.6 1.9 collective-permute-start.6
  759.5 0.7 iota_compare_fusion
  760.2 4.3 collective-permute-done.6
  764.5 1.9 collective-permute-start.3
  766.4 0.6 iota_compare_fusion.1
  767.0 4.5 collective-permute-done.3
  771.5 22.4 %collective-permute-start = (s32[1]{0:T(128)}, s32[1]{0:T(128)}, u32[]{:S(2)}, u32[]{:S(2)}) collective-permute-start(s32[1]{0:T(128)} %param.5), channel_id=1, source_target_pairs={{1,0},{2,1},{3,2},{4,3},{5,4},{6,5},{7,6},{8,7},{9,8},{10,9},{11,1... | collective-permute-start | bytes 20 | tf_op jit(solution)/shard_map/ppermute | solution.py:12
  793.9 0.7 iota_compare_fusion.2
  794.6 0.7 collective-permute-done
  795.3 15.6 %collective-permute-start.1 = (s32[768]{0:T(1024)S(1)}, s32[768]{0:T(1024)S(1)}, u32[]{:S(2)}, u32[]{:S(2)}) collective-permute-start(s32[768]{0:T(1024)S(1)} %copy-done.1), channel_id=1, source_target_pairs={{1,0},{2,1},{3,2},{4,3},{5,4},{6,5},{7,6},{8,7},{9,8},{10,9},{11,1... | collective-permute-start | bytes 9224 | tf_op jit(solution)/shard_map/ppermute | solution.py:12
  810.9 0.6 iota_compare_fusion.3
  811.5 1.9 collective-permute-start.10
  813.4 1.4 fusion.3
  814.9 1.9 collective-permute-start.4
  816.8 1.4 fusion.4
  818.2 9.0 %collective-permute-start.7 = (s32[768]{0:T(1024)S(1)}, s32[768]{0:T(1024)S(1)}, u32[]{:S(2)}, u32[]{:S(2)}) collective-permute-start(s32[768]{0:T(1024)S(1)} %copy-done.1), channel_id=1, source_target_pairs={{3,0},{4,1},{5,2},{6,3},{7,4},{8,5},{9,6},{10,7},{11,8},{12,9},{13... | collective-permute-start | bytes 9224 | tf_op jit(solution)/shard_map/ppermute | solution.py:12
  827.2 1.4 fusion.2
  828.7 5.6 select_reduce_fusion.7
  834.3 7.4 collective-permute-start.12
  841.7 5.1 collective-permute-start.13
  846.8 15.0 %collective-permute-start.14 = (f32[768]{0:T(1024)S(1)}, f32[768]{0:T(1024)S(1)}, u32[]{:S(2)}, u32[]{:S(2)}) collective-permute-start(f32[768]{0:T(1024)S(1)} %get-tuple-element.15), channel_id=1, source_target_pairs={{509,0},{510,1},{511,2},{0,3},{1,4},{2,5},{3,6},{4,7},{5,8},{6,9},... | collective-permute-start | bytes 9224 | tf_op jit(solution)/shard_map/ppermute | solution.py:18
  861.9 1.9 collective-permute-start.15
  863.8 1.6 select_reduce_fusion.8
  865.4 11.3 %collective-permute-done.15 = f32[768]{0:T(1024)S(1)} collective-permute-done((f32[768]{0:T(1024)S(1)}, f32[768]{0:T(1024)S(1)}, u32[]{:S(2)}, u32[]{:S(2)}) %collective-permute-start.15) | collective-permute-done | bytes 3104 | tf_op jit(solution)/shard_map/ppermute | solution.py:18
  876.7 0.6 maximum_maximum_fusion
  (18 shorter events, 0.4 us)
Async XLA Ops:
  0.0 1.9 copy-start
  1.9 793.4 %copy-start.1 = (s32[768]{0:T(1024)S(1)}, s32[768]{0:T(1024)}, u32[]{:S(2)}) copy-start(s32[768]{0:T(1024)} %param.4) | copy-start | bytes 9220
  2.3 809.2 %collective-permute-start.8 = (bf16[768,1024]{1,0:T(8,128)(2,1)S(1)}, bf16[768,1024]{1,0:T(8,128)(2,1)S(1)}, u32[]{:S(2)}, u32[]{:S(2)}) collective-permute-start(bf16[768,1024]{1,0:T(8,128)(2,1)S(1)} %fusion.1), channel_id=1, source_target_pairs={{3,0},{4,1},{5,2},{6,3},{7,4},{8,5},{9,6},{10,7},{11,8},{12,9},{13... | collective-permute-start | bytes 4718600 | tf_op jit(solution)/shard_map/ppermute | solution.py:12
  12.7 802.2 %collective-permute-start.11 = (bf16[768,1024]{1,0:T(8,128)(2,1)S(1)}, bf16[768,1024]{1,0:T(8,128)(2,1)S(1)}, u32[]{:S(2)}, u32[]{:S(2)}) collective-permute-start(bf16[768,1024]{1,0:T(8,128)(2,1)S(1)} %fusion.1), channel_id=1, source_target_pairs={{4,0},{5,1},{6,2},{7,3},{8,4},{9,5},{10,6},{11,7},{12,8},{13,9},{1... | collective-permute-start | bytes 4718600 | tf_op jit(solution)/shard_map/ppermute | solution.py:12
  17.9 800.4 %collective-permute-start.5 = (bf16[768,1024]{1,0:T(8,128)(2,1)S(1)}, bf16[768,1024]{1,0:T(8,128)(2,1)S(1)}, u32[]{:S(2)}, u32[]{:S(2)}) collective-permute-start(bf16[768,1024]{1,0:T(8,128)(2,1)S(1)} %fusion.1), channel_id=1, source_target_pairs={{2,0},{3,1},{4,2},{5,3},{6,4},{7,5},{8,6},{9,7},{10,8},{11,9},{12,... | collective-permute-start | bytes 4718600 | tf_op jit(solution)/shard_map/ppermute | solution.py:12
  29.3 799.4 %collective-permute-start.2 = (bf16[768,1024]{1,0:T(8,128)(2,1)S(1)}, bf16[768,1024]{1,0:T(8,128)(2,1)S(1)}, u32[]{:S(2)}, u32[]{:S(2)}) collective-permute-start(bf16[768,1024]{1,0:T(8,128)(2,1)S(1)} %fusion.1), channel_id=1, source_target_pairs={{1,0},{2,1},{3,2},{4,3},{5,4},{6,5},{7,6},{8,7},{9,8},{10,9},{11,1... | collective-permute-start | bytes 4718600 | tf_op jit(solution)/shard_map/ppermute | solution.py:12
  32.3 725.3 %collective-permute-start.9 = (s32[1]{0:T(128)}, s32[1]{0:T(128)}, u32[]{:S(2)}, u32[]{:S(2)}) collective-permute-start(s32[1]{0:T(128)} %param.5), channel_id=1, source_target_pairs={{4,0},{5,1},{6,2},{7,3},{8,4},{9,5},{10,6},{11,7},{12,8},{13,9},{1... | collective-permute-start | bytes 20 | tf_op jit(solution)/shard_map/ppermute | solution.py:12
  757.6 6.9 collective-permute-start.6
  764.5 7.0 collective-permute-start.3
  771.5 23.8 %collective-permute-start = (s32[1]{0:T(128)}, s32[1]{0:T(128)}, u32[]{:S(2)}, u32[]{:S(2)}) collective-permute-start(s32[1]{0:T(128)} %param.5), channel_id=1, source_target_pairs={{1,0},{2,1},{3,2},{4,3},{5,4},{6,5},{7,6},{8,7},{9,8},{10,9},{11,1... | collective-permute-start | bytes 20 | tf_op jit(solution)/shard_map/ppermute | solution.py:12
  795.3 33.3 %collective-permute-start.1 = (s32[768]{0:T(1024)S(1)}, s32[768]{0:T(1024)S(1)}, u32[]{:S(2)}, u32[]{:S(2)}) collective-permute-start(s32[768]{0:T(1024)S(1)} %copy-done.1), channel_id=1, source_target_pairs={{1,0},{2,1},{3,2},{4,3},{5,4},{6,5},{7,6},{8,7},{9,8},{10,9},{11,1... | collective-permute-start | bytes 9224 | tf_op jit(solution)/shard_map/ppermute | solution.py:12
  811.5 17.2 %collective-permute-start.10 = (s32[768]{0:T(1024)S(1)}, s32[768]{0:T(1024)S(1)}, u32[]{:S(2)}, u32[]{:S(2)}) collective-permute-start(s32[768]{0:T(1024)S(1)} %copy-done.1), channel_id=1, source_target_pairs={{4,0},{5,1},{6,2},{7,3},{8,4},{9,5},{10,6},{11,7},{12,8},{13,9},{1... | collective-permute-start | bytes 9224 | tf_op jit(solution)/shard_map/ppermute | solution.py:12
  814.9 13.8 %collective-permute-start.4 = (s32[768]{0:T(1024)S(1)}, s32[768]{0:T(1024)S(1)}, u32[]{:S(2)}, u32[]{:S(2)}) collective-permute-start(s32[768]{0:T(1024)S(1)} %copy-done.1), channel_id=1, source_target_pairs={{2,0},{3,1},{4,2},{5,3},{6,4},{7,5},{8,6},{9,7},{10,8},{11,9},{12,... | collective-permute-start | bytes 9224 | tf_op jit(solution)/shard_map/ppermute | solution.py:12
  818.2 10.5 %collective-permute-start.7 = (s32[768]{0:T(1024)S(1)}, s32[768]{0:T(1024)S(1)}, u32[]{:S(2)}, u32[]{:S(2)}) collective-permute-start(s32[768]{0:T(1024)S(1)} %copy-done.1), channel_id=1, source_target_pairs={{3,0},{4,1},{5,2},{6,3},{7,4},{8,5},{9,6},{10,7},{11,8},{12,9},{13... | collective-permute-start | bytes 9224 | tf_op jit(solution)/shard_map/ppermute | solution.py:12
  834.3 31.1 %collective-permute-start.12 = (f32[768]{0:T(1024)S(1)}, f32[768]{0:T(1024)S(1)}, u32[]{:S(2)}, u32[]{:S(2)}) collective-permute-start(f32[768]{0:T(1024)S(1)} %get-tuple-element.6), channel_id=1, source_target_pairs={{511,0},{0,1},{1,2},{2,3},{3,4},{4,5},{5,6},{6,7},{7,8},{8,9},{9,1... | collective-permute-start | bytes 9224 | tf_op jit(solution)/shard_map/ppermute | solution.py:18
  841.7 23.7 %collective-permute-start.13 = (f32[768]{0:T(1024)S(1)}, f32[768]{0:T(1024)S(1)}, u32[]{:S(2)}, u32[]{:S(2)}) collective-permute-start(f32[768]{0:T(1024)S(1)} %get-tuple-element.13), channel_id=1, source_target_pairs={{510,0},{511,1},{0,2},{1,3},{2,4},{3,5},{4,6},{5,7},{6,8},{7,9},{8... | collective-permute-start | bytes 9224 | tf_op jit(solution)/shard_map/ppermute | solution.py:18
  846.8 18.6 %collective-permute-start.14 = (f32[768]{0:T(1024)S(1)}, f32[768]{0:T(1024)S(1)}, u32[]{:S(2)}, u32[]{:S(2)}) collective-permute-start(f32[768]{0:T(1024)S(1)} %get-tuple-element.15), channel_id=1, source_target_pairs={{509,0},{510,1},{511,2},{0,3},{1,4},{2,5},{3,6},{4,7},{5,8},{6,9},... | collective-permute-start | bytes 9224 | tf_op jit(solution)/shard_map/ppermute | solution.py:18
  861.9 14.9 %collective-permute-start.15 = (f32[768]{0:T(1024)S(1)}, f32[768]{0:T(1024)S(1)}, u32[]{:S(2)}, u32[]{:S(2)}) collective-permute-start(f32[768]{0:T(1024)S(1)} %get-tuple-element.17), channel_id=1, source_target_pairs={{508,0},{509,1},{510,2},{511,3},{0,4},{1,5},{2,6},{3,7},{4,8},{5,9... | collective-permute-start | bytes 9224 | tf_op jit(solution)/shard_map/ppermute | solution.py:18
where the time goes:
time: 878 us; the launch traced here: 877 us
  waiting for transfers between devices  740 us (84%)
  starting transfers between devices  119 us (14%)
  matrix products  11.4 us (1%)
    ppermute x12, waiting for transfers between devices, passed_along(): return lax.ppermute(array, axis, pairs)  729 us
    ppermute x12, starting transfers between devices, passed_along(): return lax.ppermute(array, axis, pairs)  89.8 us
    ppermute x4, starting transfers between devices, passed_along_2(): return lax.ppermute(block, axis, route)  29.5 us
  transfers between devices with their start and end apart: 16, of which 5 were waited for; matrix products, arithmetic and copies ran while one was open for 1% of the time, Pallas kernels for 0%

commit v1 on v0

v1 whole, which is shorter than its diff:
```python
import functools

import jax
import jax.numpy as jnp
from jax import lax
from jax.experimental import pallas as pl
from jax.experimental.pallas import tpu as pltpu
from jax.sharding import PartitionSpec as P

MESH = pl.DeviceIdType.MESH
FAR = 2**30
CHUNKS = 6
STEPS = 3
SLOTS = 5
LANES = 128

PAIRS = (
    (
        ((0, 0), (0, 2), (1, 2), (0, 1), (3, 0)),
        ((0, 0), (0, 2), (3, 0), (3, 1), (4, 1)),
        ((0, 0), (0, 2), (3, 0), (3, 1), (4, 1)),
        ((0, 0), (1, 2), (3, 0), (3, 1), (3, 2)),
    ),
    (
        ((0, 0), (0, 2), (1, 2), (3, 0), (4, 0)),
        ((0, 0), (0, 2), (3, 0), (4, 0), (4, 1)),
        ((0, 0), (0, 2), (3, 0), (4, 0), (4, 1)),
        ((0, 0), (0, 2), (1, 2), (3, 0), (3, 2)),
    ),
)


def host_of(block, planes, cols):
    row, col = block // cols, block % cols
    zlo, core = row // 2, row % 2
    plane = (zlo + planes // 2 + planes * ((zlo + core) % 2)) % (2 * planes)
    half = (col // 4) % 2
    return (plane % planes) * 2 + half, (col // 8) * 8 + (plane // planes) * 4 + col % 4


def kernel(
    rows, cols, emb_ref, ids_ref, count_ref, out_ref,
    own, blk, kown, kin, kcol, rowacc, colacc, rout, rin,
    zsend, bsend, fsend, recv, ksend, krecv, rsend, rrecv,
):
    planes, total = rows // 2, rows * cols
    size, depth = emb_ref.shape
    piece = size // CHUNKS
    row, col = lax.axis_index("row"), lax.axis_index("col")
    me = row * cols + col
    core, y, xi, half = row % 2, col % 4, col // 8, (col // 4) % 2
    level = (half * planes + row // 2 + 2 * planes - planes // 2) % (2 * planes)
    held_core = (level % planes + level // planes) % 2
    held = ((level % planes) * 2 + held_core) * cols + xi * 8 + core * 4 + y

    def host(block):
        return host_of(block, planes, cols)

    def home(block):
        return block // cols, block % cols

    has_next = me + 4 < total
    needed = (
        host(me),
        host(me - y + (y + 1) % 4),
        host(me - y + (y + 3) % 4),
        host(me + 4),
        host(me + 3),
    )
    needed_if = (None, None, None, has_next, has_next & (y >= 1 + half))
    homes = (
        home(held),
        home(held - y + (y + 3) % 4),
        home(held - y + (y + 1) % 4),
        home(held - 4),
        home(held - 3),
    )
    has_before = held >= 4
    homes_if = (None, None, None, has_before, has_before & (y <= 2) & (y >= 1 - core))
    crossing = (xi == cols // 8 - 1) & (half == 1) & (core == 0)
    up, down = host(held - y + (y + 1) % 4), host(held - y + (y + 3) % 4)
    after, before = host(held + 4), host(held - 4)
    has_after = held + 4 < total
    held_crossing = (core == 1) & (xi == cols // 8 - 1) & (held_core == 0)

    def when(condition, act):
        if condition is None:
            act()
        else:
            pl.when(condition)(act)

    barrier = pltpu.get_barrier_semaphore()

    def greet(device):
        pl.semaphore_signal(barrier, inc=1, device_id=device, device_id_type=MESH)

    for slot in range(SLOTS):
        when(needed_if[slot], functools.partial(greet, needed[slot]))
        when(homes_if[slot], functools.partial(greet, homes[slot]))
    greet(up)
    greet(down)
    when(has_after, functools.partial(greet, after))
    when(has_before, functools.partial(greet, before))

    def one(condition):
        return condition.astype(jnp.int32)

    greetings = (
        8
        + one(needed_if[3]) + one(needed_if[4]) + one(homes_if[3]) + one(homes_if[4])
        + one(has_after) + one(has_before)
    )

    places = lax.broadcasted_iota(jnp.int32, (1, size), 1)
    valid = places < count_ref[0]
    kown[...] = jnp.where(valid, ids_ref[...], FAR)
    rowacc[...] = jnp.full(rowacc.shape, -1.0, jnp.float32)
    colacc[...] = jnp.full(colacc.shape, -1.0, jnp.float32)
    pl.semaphore_wait(barrier, greetings)

    def key_copy(slot):
        return pltpu.make_async_remote_copy(
            src_ref=kown, dst_ref=kin.at[slot], send_sem=ksend.at[slot], recv_sem=krecv.at[slot],
            device_id=needed[slot], device_id_type=MESH,
        )

    def result_copy(slot):
        return pltpu.make_async_remote_copy(
            src_ref=rout.at[slot], dst_ref=rin.at[slot], send_sem=rsend.at[slot], recv_sem=rrecv.at[slot],
            device_id=homes[slot], device_id_type=MESH,
        )

    def part(c):
        return pl.ds(pl.multiple_of(c * piece, piece), piece)

    def first_copy(c, slot, sems):
        return pltpu.make_async_remote_copy(
            src_ref=own.at[part(c)], dst_ref=blk.at[slot, part(c)], send_sem=sems.at[c],
            recv_sem=recv.at[slot, c], device_id=needed[slot], device_id_type=MESH,
        )

    def forward(c, way, source, target, device):
        return pltpu.make_async_remote_copy(
            src_ref=blk.at[source, part(c)], dst_ref=blk.at[target, part(c)], send_sem=fsend.at[way, c],
            recv_sem=recv.at[target, c], device_id=device, device_id_type=MESH,
        )

    forwards = (
        (0, 0, 1, up, None),
        (1, 0, 2, down, None),
        (2, 0, 3, after, has_after & jnp.logical_not(held_crossing)),
        (3, 2, 4, after, (core == 0) & (y <= 2)),
        (4, 3, 4, down, (core == 0) & (y >= 2) & has_before),
    )

    for slot in range(SLOTS):
        when(needed_if[slot], lambda slot=slot: key_copy(slot).start())

    @pl.loop(0, CHUNKS)
    def _(c):
        floats = emb_ref[part(c), :].astype(jnp.float32)
        sums = jnp.sum(floats * floats, axis=-1, keepdims=True)
        own[part(c), :] = (floats * lax.rsqrt(sums + 1e-06)).astype(jnp.bfloat16)
        first_copy(c, 0, zsend).start()
        pl.when(crossing)(lambda: first_copy(c, 3, bsend).start())

    for slot in range(SLOTS):

        @functools.partial(when, homes_if[slot])
        def _(slot=slot):
            key_copy(slot).wait_recv()
            for g in range(size // LANES):
                lanes = slice(g * LANES, (g + 1) * LANES)
                kcol[slot, lanes, :] = jnp.broadcast_to(kin[slot, :, lanes], (LANES, LANES)).T

    lefts, rights = [], []
    for p in range(SLOTS):
        for side, kept in ((0, lefts), (1, rights)):
            value = jnp.int32(PAIRS[0][0][p][side])
            for k in range(2):
                for j in range(4):
                    other = PAIRS[k][j][p][side]
                    value = jnp.where((core == k) & (y == j), other, value)
            kept.append(value)
    skipped = jnp.where(y == 0, 1, 3)
    pairs = jnp.where(has_before, SLOTS, SLOTS - skipped)

    def pick(values, p):
        value = values[0]
        for k in range(1, SLOTS):
            value = jnp.where(p == k, values[k], value)
        return value

    def tile(left, right, i, count, j, width):
        scores = lax.dot_general(
            blk[left, i : i + count, :], blk[right, j : j + width, :],
            (((1,), (1,)), ((), ())), preferred_element_type=jnp.float32,
        )
        mine = kcol[left, i : i + count, :]
        best = rowacc[left, i : i + count, :]
        for g in range(width // LANES):
            lanes = slice(j + g * LANES, j + (g + 1) * LANES)
            part_scores = scores[:, g * LANES : (g + 1) * LANES]
            theirs = kin[right, :, lanes]
            best = jnp.maximum(best, jnp.where(theirs < mine, part_scores, -1.0))
            upper = jnp.where(mine < theirs, part_scores, -1.0)
            upper = jnp.max(upper.reshape(count // 8, 8, LANES), axis=0)
            colacc[right, :, lanes] = jnp.maximum(colacc[right, :, lanes], upper)
        rowacc[left, i : i + count, :] = best

    step = size // STEPS
    for k in range(STEPS):

        @pl.loop(k * CHUNKS // STEPS, (k + 1) * CHUNKS // STEPS)
        def _(c):
            for slot in range(SLOTS):

                @functools.partial(when, homes_if[slot])
                def _(slot=slot):
                    forward(c, 0, slot, slot, up).wait_recv()

                for way, source, target, device, condition in forwards:
                    if source == slot:
                        when(condition, lambda: forward(c, way, source, target, device).start())

        @pl.loop(0, pairs)
        def _(p):
            left, right = pick(lefts, p), pick(rights, p)
            tile(left, right, k * step, step, 0, (k + 1) * step)
            for i in range(k):
                tile(left, right, i * step, step, k * step, step)

    for slot in (3, 4, 1, 2, 0):

        @functools.partial(when, homes_if[slot])
        def _(slot=slot):
            best = jnp.max(colacc[slot], axis=0, keepdims=True)
            for g in range(size // LANES):
                lanes = slice(g * LANES, (g + 1) * LANES)
                across = jnp.max(rowacc[slot, lanes, :].T, axis=0, keepdims=True)
                rout[slot, :, lanes] = jnp.maximum(best[:, lanes], across)
            result_copy(slot).start()

    @pl.loop(0, CHUNKS)
    def _(c):
        first_copy(c, 0, zsend).wait_send()
        pl.when(crossing)(lambda: first_copy(c, 3, bsend).wait_send())
        for way, source, target, device, condition in forwards:
            when(condition, lambda: forward(c, way, source, target, device).wait_send())

    for slot in range(SLOTS):
        when(needed_if[slot], lambda slot=slot: key_copy(slot).wait_send())

    for slot in range(SLOTS):

        @functools.partial(when, needed_if[slot])
        def _(slot=slot):
            result_copy(slot).wait_recv()
            if slot == 0:
                out_ref[...] = rin[slot]
            else:
                out_ref[...] = jnp.maximum(out_ref[...], rin[slot])

    out_ref[...] = jnp.where(valid, out_ref[...], -1.0)
    for slot in range(SLOTS):
        when(homes_if[slot], lambda slot=slot: result_copy(slot).wait_send())


def solution(mesh):
    rows, cols = mesh.shape["row"], mesh.shape["col"]

    def local(embeddings, doc_ids, valid_counts):
        size, depth = embeddings.shape
        vmem = pl.BlockSpec(memory_space=pltpu.VMEM)
        nearest = pl.pallas_call(
            functools.partial(kernel, rows, cols),
            out_shape=jax.ShapeDtypeStruct((1, size), jnp.float32),
            in_specs=[vmem, vmem, pl.BlockSpec(memory_space=pltpu.SMEM)],
            out_specs=vmem,
            scratch_shapes=[
                pltpu.VMEM((size, depth), jnp.bfloat16),
                pltpu.VMEM((SLOTS, size, depth), jnp.bfloat16),
                pltpu.VMEM((1, size), jnp.int32),
                pltpu.VMEM((SLOTS, 1, size), jnp.int32),
                pltpu.VMEM((SLOTS, size, LANES), jnp.int32),
                pltpu.VMEM((SLOTS, size, LANES), jnp.float32),
                pltpu.VMEM((SLOTS, 8, size), jnp.float32),
                pltpu.VMEM((SLOTS, 1, size), jnp.float32),
                pltpu.VMEM((SLOTS, 1, size), jnp.float32),
                pltpu.SemaphoreType.DMA((CHUNKS,)),
                pltpu.SemaphoreType.DMA((CHUNKS,)),
                pltpu.SemaphoreType.DMA((SLOTS, CHUNKS)),
                pltpu.SemaphoreType.DMA((SLOTS, CHUNKS)),
                pltpu.SemaphoreType.DMA((SLOTS,)),
                pltpu.SemaphoreType.DMA((SLOTS,)),
                pltpu.SemaphoreType.DMA((SLOTS,)),
                pltpu.SemaphoreType.DMA((SLOTS,)),
            ],
            compiler_params=pltpu.CompilerParams(
                collective_id=0, has_side_effects=True, vmem_limit_bytes=48 * 2**20
            ),
            cost_estimate=pl.CostEstimate(
                flops=10 * size * size * depth, bytes_accessed=4 * size * depth, transcendentals=0
            ),
        )(embeddings, doc_ids.reshape(1, size), valid_counts)
        return nearest.reshape(size)

    in_specs = (P(("row", "col"), None), P(("row", "col")), P(("row", "col")))
    return jax.shard_map(
        local, mesh=mesh, in_specs=in_specs, out_specs=P(("row", "col")), check_vma=False
    )
```

time: 878 us -> 205 us (0.23)
  the two profiles are of different devices: /device:TPU:224 before, /device:TPU:32 now
where the time goes in v1:
time: 205 us
  Pallas kernels  201 us (98%)
  local copies, waits for them, and re-layouts  2.1 us (1%)
    pallas_call x1, Pallas kernels, local(): pl.pallas_call(functools.partial(kernel, rows, cols), out_shape=jax.Shape...  201 us

profile of v1, /device:TPU:32, one launch (start us, length us, event | category | flops | bytes accessed | tf_op | source)
XLA Modules:
  0.0 204.8 jit_solution(9266720627409386496)
XLA Ops:
  0.7 0.7 reshape.6.ids_ref
  1.3 0.0 copy-start
  1.3 1.4 copy-done
  2.8 201.4 %shard_map.37 = f32[1,768]{1,0:T(1,128)S(1)} custom-call(bf16[768,1024]{1,0:T(8,128)(2,1)S(1)} %copy-done, s32[1,768]{1,0:T(1,128)S(1)} %reshape.6.ids_ref, s32[1]{0:T(128)S(6)} %copy.4.count_ref), custom_call_target="tpu_custom_call" | custom-call | flops 6039797760 | bytes 3145728 | tf_op jit(solution)/shard_map/pallas_call | solution.py:275
  204.2 0.6 reduce
Async XLA Ops:
  1.3 1.4 copy-start

commit v2 on v1

--- a/solution.py
+++ b/solution.py
@@ -9,25 +9,26 @@
 
 MESH = pl.DeviceIdType.MESH
 FAR = 2**30
-CHUNKS = 6
+CHUNKS = 8
 STEPS = 3
 SLOTS = 5
 LANES = 128
 
 PAIRS = (
+    (
+        ((0, 0), (0, 2), (0, 1), (3, 0), (4, 2)),
+        ((0, 0), (0, 2), (1, 2), (3, 0), (3, 1)),
+        ((0, 0), (0, 2), (1, 2), (3, 0), (3, 1)),
+        ((0, 0), (3, 0), (3, 1), (3, 2), (4, 2)),
+    ),
     (
         ((0, 0), (0, 2), (1, 2), (0, 1), (3, 0)),
         ((0, 0), (0, 2), (3, 0), (3, 1), (4, 1)),
         ((0, 0), (0, 2), (3, 0), (3, 1), (4, 1)),
         ((0, 0), (1, 2), (3, 0), (3, 1), (3, 2)),
     ),
-    (
-        ((0, 0), (0, 2), (1, 2), (3, 0), (4, 0)),
-        ((0, 0), (0, 2), (3, 0), (4, 0), (4, 1)),
-        ((0, 0), (0, 2), (3, 0), (4, 0), (4, 1)),
-        ((0, 0), (0, 2), (1, 2), (3, 0), (3, 2)),
-    ),
 )
+AHEAD = 3
 
 
 def host_of(block, planes, cols):
@@ -40,8 +41,8 @@
 
 def kernel(
     rows, cols, emb_ref, ids_ref, count_ref, out_ref,
-    own, blk, kown, kin, kcol, rowacc, colacc, rout, rin,
-    zsend, bsend, fsend, recv, ksend, krecv, rsend, rrecv,
+    own, relayed, blk, kown, kin, kcol, rowacc, colacc, rout, rin,
+    zsend, bsend, msend, mrecv, fsend, recv, ksend, krecv, rsend, rrecv,
 ):
     planes, total = rows // 2, rows * cols
     size, depth = emb_ref.shape
@@ -65,29 +66,43 @@
         host(me - y + (y + 1) % 4),
         host(me - y + (y + 3) % 4),
         host(me + 4),
-        host(me + 3),
+        host(me + 4 - half * (y - (y + 1) % 4) - (1 - half)),
     )
-    needed_if = (None, None, None, has_next, has_next & (y >= 1 + half))
+    needed_if = (None, None, None, has_next, has_next & (y >= 2))
     homes = (
         home(held),
         home(held - y + (y + 3) % 4),
         home(held - y + (y + 1) % 4),
         home(held - 4),
-        home(held - 3),
+        home(held - 4 + core - (1 - core) * (y - (y + 3) % 4)),
     )
     has_before = held >= 4
-    homes_if = (None, None, None, has_before, has_before & (y <= 2) & (y >= 1 - core))
-    crossing = (xi == cols // 8 - 1) & (half == 1) & (core == 0)
+    far_in = jnp.where(core == 0, (y == 0) | (y == 3), (y == 1) | (y == 2))
+    homes_if = (None, None, None, has_before, has_before & far_in)
+    routes = cols // 8
+    last = routes - 1
+    crossing = (xi == last) & (half == 1) & (core == 0)
+    leaving = (xi == last) & (core == 1) & (held_core == 1) & (held + 4 < total)
+    relay_first = (xi < last) & (half == 1) & (core == 0)
+    relay_next = held + (last - xi) * 8 + 4
+    relay_later = (xi < last) & (core == 1) & (held_core == 1) & (relay_next < total)
+    relay = relay_first | relay_later
+    relay_to = host(jnp.where(core == 0, me + (last - xi) * 8 + 4, relay_next))
+    entering = (core == 0) & (xi == 0) & has_before
     up, down = host(held - y + (y + 1) % 4), host(held - y + (y + 3) % 4)
     after, before = host(held + 4), host(held - 4)
+    far = host(held + 4 - core * (y - (y + 1) % 4) - (1 - core))
     has_after = held + 4 < total
-    held_crossing = (core == 1) & (xi == cols // 8 - 1) & (held_core == 0)
+    passes = has_after & jnp.logical_not((core == 1) & (xi == last))
 
     def when(condition, act):
         if condition is None:
             act()
         else:
             pl.when(condition)(act)
+
+    def one_if(condition):
+        return condition.astype(jnp.int32)
 
     barrier = pltpu.get_barrier_semaphore()
 
@@ -101,14 +116,28 @@
     greet(down)
     when(has_after, functools.partial(greet, after))
     when(has_before, functools.partial(greet, before))
-
-    def one(condition):
-        return condition.astype(jnp.int32)
+    greet_far_from = host(held - 4 + core - (1 - core) * (y - (y + 3) % 4))
+    when(passes & (y >= 2), functools.partial(greet, far))
+    far_from = homes_if[4] & jnp.logical_not(entering)
+    when(far_from, functools.partial(greet, greet_far_from))
+
+    def lane(k):
+        return row, col - (xi - k) * 8
+
+    for k in range(last):
+        when(crossing | leaving, functools.partial(greet, lane(k)))
+    when(relay, functools.partial(greet, lane(last)))
+    when(relay, functools.partial(greet, relay_to))
+    entry_row = jnp.where(held_core == 1, homes[3][0], before[0])
+    entry_col = jnp.where(held_core == 1, homes[3][1], before[1])
+    for k in range(last):
+        when(entering, functools.partial(greet, (entry_row, entry_col - (last - k) * 8)))
 
     greetings = (
         8
-        + one(needed_if[3]) + one(needed_if[4]) + one(homes_if[3]) + one(homes_if[4])
-        + one(has_after) + one(has_before)
+        + one_if(needed_if[3]) + one_if(needed_if[4]) + one_if(homes_if[3]) + one_if(homes_if[4])
+        + one_if(has_after) + one_if(has_before) + one_if(passes & (y >= 2)) + one_if(far_from)
+        + last * one_if(crossing | leaving) + 2 * one_if(relay) + last * one_if(entering)
     )
 
     places = lax.broadcasted_iota(jnp.int32, (1, size), 1)
@@ -148,10 +177,25 @@
     forwards = (
         (0, 0, 1, up, None),
         (1, 0, 2, down, None),
-        (2, 0, 3, after, has_after & jnp.logical_not(held_crossing)),
-        (3, 2, 4, after, (core == 0) & (y <= 2)),
-        (4, 3, 4, down, (core == 0) & (y >= 2) & has_before),
+        (2, 0, 3, after, passes),
+        (3, 0, 4, far, passes & (y >= 2)),
     )
+    entered = (4, 3, 4, up)
+    entered_on = entering & (y >= 2)
+
+    def relay_in(c, source):
+        k, turn = c % routes, c // routes
+        return pltpu.make_async_remote_copy(
+            src_ref=source.at[part(c)], dst_ref=relayed.at[turn], send_sem=bsend.at[c],
+            recv_sem=mrecv.at[turn], device_id=(row, col - (xi - k) * 8), device_id_type=MESH,
+        )
+
+    def relay_out(turn):
+        c = turn * routes + xi
+        return pltpu.make_async_remote_copy(
+            src_ref=relayed.at[turn], dst_ref=blk.at[3, part(c)], send_sem=msend.at[turn],
+            recv_sem=recv.at[3, c], device_id=relay_to, device_id_type=MESH,
+        )
 
     for slot in range(SLOTS):
         when(needed_if[slot], lambda slot=slot: key_copy(slot).start())
@@ -161,8 +205,9 @@
         floats = emb_ref[part(c), :].astype(jnp.float32)
         sums = jnp.sum(floats * floats, axis=-1, keepdims=True)
         own[part(c), :] = (floats * lax.rsqrt(sums + 1e-06)).astype(jnp.bfloat16)
-        first_copy(c, 0, zsend).start()
-        pl.when(crossing)(lambda: first_copy(c, 3, bsend).start())
+        pl.when(c < 2)(lambda: first_copy(c, 0, zsend).start())
+        pl.when(crossing & (c % routes == last))(lambda: first_copy(c, 3, bsend).start())
+        pl.when(crossing & (c % routes != last))(lambda: relay_in(c, own).start())
 
     for slot in range(SLOTS):
 
@@ -172,6 +217,13 @@
             for g in range(size // LANES):
                 lanes = slice(g * LANES, (g + 1) * LANES)
                 kcol[slot, lanes, :] = jnp.broadcast_to(kin[slot, :, lanes], (LANES, LANES)).T
+
+    for turn in range(CHUNKS // routes):
+
+        @pl.when(relay_first)
+        def _(turn=turn):
+            relay_in(turn * routes, own).wait_recv()
+            relay_out(turn).start()
 
     lefts, rights = [], []
     for p in range(SLOTS):
@@ -182,7 +234,7 @@
                     other = PAIRS[k][j][p][side]
                     value = jnp.where((core == k) & (y == j), other, value)
             kept.append(value)
-    skipped = jnp.where(y == 0, 1, 3)
+    skipped = jnp.where(y == 3, 4, 2)
     pairs = jnp.where(has_before, SLOTS, SLOTS - skipped)
 
     def pick(values, p):
@@ -209,19 +261,45 @@
         rowacc[left, i : i + count, :] = best
 
     step = size // STEPS
+
+    def advance(c):
+        forward(c, 0, 0, 0, up).wait_recv()
+        for way, source, target, device, condition in forwards:
+            when(condition, lambda: forward(c, way, source, target, device).start())
+        pl.when(leaving & (c % routes == last))(lambda: forward(c, 2, 0, 3, after).start())
+        pl.when(leaving & (c % routes != last))(lambda: relay_in(c, blk.at[0]).start())
+
+    def pass_on(c):
+        @pl.when(relay_later & (c % routes == xi))
+        def _():
+            relay_in(c, own).wait_recv()
+            relay_out(c // routes).start()
+
+    def enter(c):
+        @pl.when(entered_on)
+        def _():
+            forward(c, 0, 3, 3, up).wait_recv()
+            forward(c, *entered).start()
+
+    def arrive(c):
+        for slot in range(1, SLOTS):
+            condition = homes_if[slot]
+            if slot == 3:
+                condition = condition & jnp.logical_not(entered_on)
+            when(condition, lambda: forward(c, 0, slot, slot, up).wait_recv())
+
+    need = [-(-(k + 1) * step // piece) for k in range(STEPS)]
+    ahead = [min(n + AHEAD, CHUNKS + 2) for n in need[:-1]] + [CHUNKS + 2]
     for k in range(STEPS):
 
-        @pl.loop(k * CHUNKS // STEPS, (k + 1) * CHUNKS // STEPS)
-        def _(c):
-            for slot in range(SLOTS):
-
-                @functools.partial(when, homes_if[slot])
-                def _(slot=slot):
-                    forward(c, 0, slot, slot, up).wait_recv()
-
-                for way, source, target, device, condition in forwards:
-                    if source == slot:
-                        when(condition, lambda: forward(c, way, source, target, device).start())
+        @pl.loop(ahead[k - 1] if k else 0, ahead[k])
+        def _(i):
+            pl.when(i < CHUNKS)(lambda: advance(i))
+            pl.when(i + 2 < CHUNKS)(lambda: first_copy(i + 2, 0, zsend).start())
+            pl.when((i >= 1) & (i <= CHUNKS))(lambda: pass_on(i - 1))
+            pl.when(i >= 2)(lambda: enter(i - 2))
+
+        pl.loop(need[k - 1] if k else 0, need[k])(arrive)
 
         @pl.loop(0, pairs)
         def _(p):
@@ -234,20 +312,33 @@
 
         @functools.partial(when, homes_if[slot])
         def _(slot=slot):
-            best = jnp.max(colacc[slot], axis=0, keepdims=True)
+            if slot < 3:
+                best = jnp.max(colacc[slot], axis=0, keepdims=True)
             for g in range(size // LANES):
                 lanes = slice(g * LANES, (g + 1) * LANES)
-                across = jnp.max(rowacc[slot, lanes, :].T, axis=0, keepdims=True)
-                rout[slot, :, lanes] = jnp.maximum(best[:, lanes], across)
+                if slot != 2:
+                    across = jnp.max(rowacc[slot, lanes, :].T, axis=0, keepdims=True)
+                if slot > 2:
+                    rout[slot, :, lanes] = across
+                elif slot == 2:
+                    rout[slot, :, lanes] = best[:, lanes]
+                else:
+                    rout[slot, :, lanes] = jnp.maximum(best[:, lanes], across)
             result_copy(slot).start()
 
     @pl.loop(0, CHUNKS)
     def _(c):
         first_copy(c, 0, zsend).wait_send()
-        pl.when(crossing)(lambda: first_copy(c, 3, bsend).wait_send())
+        pl.when(crossing & (c % routes == last))(lambda: first_copy(c, 3, bsend).wait_send())
+        pl.when(crossing & (c % routes != last))(lambda: relay_in(c, own).wait_send())
+        pl.when(leaving & (c % routes == last))(lambda: forward(c, 2, 0, 3, after).wait_send())
+        pl.when(leaving & (c % routes != last))(lambda: relay_in(c, blk.at[0]).wait_send())
+        pl.when(entered_on)(lambda: forward(c, *entered).wait_send())
         for way, source, target, device, condition in forwards:
             when(condition, lambda: forward(c, way, source, target, device).wait_send())
 
+    for turn in range(CHUNKS // routes):
+        pl.when(relay)(lambda turn=turn: relay_out(turn).wait_send())
     for slot in range(SLOTS):
         when(needed_if[slot], lambda slot=slot: key_copy(slot).wait_send())
 
@@ -268,6 +359,7 @@
 
 def solution(mesh):
     rows, cols = mesh.shape["row"], mesh.shape["col"]
+    routes = cols // 8
 
     def local(embeddings, doc_ids, valid_counts):
         size, depth = embeddings.shape
@@ -279,6 +371,7 @@
             out_specs=vmem,
             scratch_shapes=[
                 pltpu.VMEM((size, depth), jnp.bfloat16),
+                pltpu.VMEM((CHUNKS // routes, size // CHUNKS, depth), jnp.bfloat16),
                 pltpu.VMEM((SLOTS, size, depth), jnp.bfloat16),
                 pltpu.VMEM((1, size), jnp.int32),
                 pltpu.VMEM((SLOTS, 1, size), jnp.int32),
@@ -289,6 +382,8 @@
                 pltpu.VMEM((SLOTS, 1, size), jnp.float32),
                 pltpu.SemaphoreType.DMA((CHUNKS,)),
                 pltpu.SemaphoreType.DMA((CHUNKS,)),
+                pltpu.SemaphoreType.DMA((CHUNKS // routes,)),
+                pltpu.SemaphoreType.DMA((CHUNKS // routes,)),
                 pltpu.SemaphoreType.DMA((SLOTS, CHUNKS)),
                 pltpu.SemaphoreType.DMA((SLOTS, CHUNKS)),
                 pltpu.SemaphoreType.DMA((SLOTS,)),

time: 205 us -> 129 us (0.63)
  Pallas kernels: 201 us -> 126 us
    pallas_call x1, Pallas kernels: 201 us -> 126 us  [local(): pl.pallas_call(functools.partial(kernel, rows, cols), out_shape=jax.Shape...]
where the time goes in v2:
time: 129 us
  Pallas kernels  126 us (98%)
  local copies, waits for them, and re-layouts  2.1 us (2%)
    pallas_call x1, Pallas kernels, local(): pl.pallas_call(functools.partial(kernel, rows, cols), out_shape=jax.Shape...  126 us

profile of v2, /device:TPU:32, one launch (start us, length us, event | category | flops | bytes accessed | tf_op | source)
XLA Modules:
  0.0 129.0 jit_solution(6068773174703173891)
XLA Ops:
  0.7 0.7 reshape.6.ids_ref
  1.3 0.0 copy-start
  1.3 1.4 %copy-done = bf16[768,1024]{1,0:T(8,128)(2,1)S(1)} copy-done((bf16[768,1024]{1,0:T(8,128)(2,1)S(1)}, bf16[768,1024]{1,0:T(8,128)(2,1)}, u32[]{:S(2)}) %copy-start) | copy-done | bytes 1572888
  2.8 125.6 %shard_map.37 = f32[1,768]{1,0:T(1,128)S(1)} custom-call(bf16[768,1024]{1,0:T(8,128)(2,1)S(1)} %copy-done, s32[1,768]{1,0:T(1,128)S(1)} %reshape.6.ids_ref, s32[1]{0:T(128)S(6)} %copy.4.count_ref), custom_call_target="tpu_custom_call" | custom-call | flops 6039797760 | bytes 3145728 | tf_op jit(solution)/shard_map/pallas_call | solution.py:367
  128.4 0.6 reduce
Async XLA Ops:
  1.3 1.4 %copy-start = (bf16[768,1024]{1,0:T(8,128)(2,1)S(1)}, bf16[768,1024]{1,0:T(8,128)(2,1)}, u32[]{:S(2)}) copy-start(bf16[768,1024]{1,0:T(8,128)(2,1)} %emb_ref.1) | copy-start | bytes 4718596

commit v3 on v2

--- a/solution.py
+++ b/solution.py
@@ -9,7 +9,7 @@
 
 MESH = pl.DeviceIdType.MESH
 FAR = 2**30
-CHUNKS = 8
+CHUNKS = 12
 STEPS = 3
 SLOTS = 5
 LANES = 128
@@ -28,7 +28,7 @@
         ((0, 0), (1, 2), (3, 0), (3, 1), (3, 2)),
     ),
 )
-AHEAD = 3
+FLYING = 3
 
 
 def host_of(block, planes, cols):
@@ -40,12 +40,12 @@
 
 
 def kernel(
-    rows, cols, emb_ref, ids_ref, count_ref, out_ref,
-    own, relayed, blk, kown, kin, kcol, rowacc, colacc, rout, rin,
+    rows, cols, emb_hbm, ids_ref, count_ref, out_ref,
+    emb_ref, esem, own, relayed, blk, kown, kin, kcol, rowacc, colacc, rout, rin,
     zsend, bsend, msend, mrecv, fsend, recv, ksend, krecv, rsend, rrecv,
 ):
     planes, total = rows // 2, rows * cols
-    size, depth = emb_ref.shape
+    size, depth = emb_hbm.shape
     piece = size // CHUNKS
     row, col = lax.axis_index("row"), lax.axis_index("col")
     me = row * cols + col
@@ -106,6 +106,13 @@
 
     barrier = pltpu.get_barrier_semaphore()
 
+    def part(c):
+        return pl.ds(pl.multiple_of(c * piece, piece), piece)
+
+    def load(c):
+        return pltpu.make_async_copy(emb_hbm.at[part(c)], emb_ref.at[part(c)], esem.at[c])
+
+
     def greet(device):
         pl.semaphore_signal(barrier, inc=1, device_id=device, device_id_type=MESH)
 
@@ -140,9 +147,10 @@
         + last * one_if(crossing | leaving) + 2 * one_if(relay) + last * one_if(entering)
     )
 
+    pl.loop(0, CHUNKS)(lambda c: load(c).start())
     places = lax.broadcasted_iota(jnp.int32, (1, size), 1)
     valid = places < count_ref[0]
-    kown[...] = jnp.where(valid, ids_ref[...], FAR)
+    kown[...] = jnp.where(valid, ids_ref[...].reshape(1, size), FAR)
     rowacc[...] = jnp.full(rowacc.shape, -1.0, jnp.float32)
     colacc[...] = jnp.full(colacc.shape, -1.0, jnp.float32)
     pl.semaphore_wait(barrier, greetings)
@@ -158,9 +166,6 @@
             src_ref=rout.at[slot], dst_ref=rin.at[slot], send_sem=rsend.at[slot], recv_sem=rrecv.at[slot],
             device_id=homes[slot], device_id_type=MESH,
         )
-
-    def part(c):
-        return pl.ds(pl.multiple_of(c * piece, piece), piece)
 
     def first_copy(c, slot, sems):
         return pltpu.make_async_remote_copy(
@@ -202,10 +207,11 @@
 
     @pl.loop(0, CHUNKS)
     def _(c):
+        load(c).wait()
         floats = emb_ref[part(c), :].astype(jnp.float32)
         sums = jnp.sum(floats * floats, axis=-1, keepdims=True)
         own[part(c), :] = (floats * lax.rsqrt(sums + 1e-06)).astype(jnp.bfloat16)
-        pl.when(c < 2)(lambda: first_copy(c, 0, zsend).start())
+        pl.when(c < FLYING)(lambda: first_copy(c, 0, zsend).start())
         pl.when(crossing & (c % routes == last))(lambda: first_copy(c, 3, bsend).start())
         pl.when(crossing & (c % routes != last))(lambda: relay_in(c, own).start())
 
@@ -234,8 +240,8 @@
                     other = PAIRS[k][j][p][side]
                     value = jnp.where((core == k) & (y == j), other, value)
             kept.append(value)
-    skipped = jnp.where(y == 3, 4, 2)
-    pairs = jnp.where(has_before, SLOTS, SLOTS - skipped)
+    inner = jnp.where(core == 0, jnp.where(y == 3, 1, 3), jnp.where(y == 0, 4, 2))
+    pairs = jnp.where(has_before, SLOTS, inner)
 
     def pick(values, p):
         value = values[0]
@@ -281,32 +287,52 @@
             forward(c, 0, 3, 3, up).wait_recv()
             forward(c, *entered).start()
 
-    def arrive(c):
-        for slot in range(1, SLOTS):
-            condition = homes_if[slot]
-            if slot == 3:
-                condition = condition & jnp.logical_not(entered_on)
-            when(condition, lambda: forward(c, 0, slot, slot, up).wait_recv())
-
-    need = [-(-(k + 1) * step // piece) for k in range(STEPS)]
-    ahead = [min(n + AHEAD, CHUNKS + 2) for n in need[:-1]] + [CHUNKS + 2]
-    for k in range(STEPS):
-
-        @pl.loop(ahead[k - 1] if k else 0, ahead[k])
+    def arrive_near(c):
+        for slot in (1, 2):
+            forward(c, 0, slot, slot, up).wait_recv()
+
+    def arrive_far(c):
+        pl.when(has_before & jnp.logical_not(entered_on))(lambda: forward(c, 0, 3, 3, up).wait_recv())
+        pl.when(homes_if[4])(lambda: forward(c, 0, 4, 4, up).wait_recv())
+
+    def go(first, end):
+        @pl.loop(first, end)
         def _(i):
             pl.when(i < CHUNKS)(lambda: advance(i))
-            pl.when(i + 2 < CHUNKS)(lambda: first_copy(i + 2, 0, zsend).start())
+            pl.when(i + FLYING < CHUNKS)(lambda: first_copy(i + FLYING, 0, zsend).start())
             pl.when((i >= 1) & (i <= CHUNKS))(lambda: pass_on(i - 1))
-            pl.when(i >= 2)(lambda: enter(i - 2))
-
-        pl.loop(need[k - 1] if k else 0, need[k])(arrive)
-
-        @pl.loop(0, pairs)
+            pl.when((i >= 2) & (i <= CHUNKS + 1))(lambda: enter(i - 2))
+
+    def near(k):
+        pl.loop(k * CHUNKS // STEPS, (k + 1) * CHUNKS // STEPS)(arrive_near)
+
+    def distant(k):
+        pl.loop(k * CHUNKS // STEPS, (k + 1) * CHUNKS // STEPS)(arrive_far)
+
+    def compute(k, first, end):
+        @pl.loop(first, end)
         def _(p):
             left, right = pick(lefts, p), pick(rights, p)
             tile(left, right, k * step, step, 0, (k + 1) * step)
-            for i in range(k):
-                tile(left, right, i * step, step, k * step, step)
+            if k:
+                tile(left, right, 0, k * step, k * step, step)
+
+    third = CHUNKS // STEPS
+    go(0, third + 4)
+    near(0)
+    distant(0)
+    compute(0, 0, pairs)
+    go(third + 4, 2 * third + 2)
+    near(1)
+    compute(1, 0, inner)
+    go(2 * third + 2, 2 * third + 4)
+    distant(1)
+    compute(1, inner, pairs)
+    go(2 * third + 4, 3 * third + 2)
+    near(2)
+    compute(2, 0, inner)
+    distant(2)
+    compute(2, inner, pairs)
 
     for slot in (3, 4, 1, 2, 0):
 
@@ -347,12 +373,10 @@
         @functools.partial(when, needed_if[slot])
         def _(slot=slot):
             result_copy(slot).wait_recv()
-            if slot == 0:
-                out_ref[...] = rin[slot]
-            else:
-                out_ref[...] = jnp.maximum(out_ref[...], rin[slot])
-
-    out_ref[...] = jnp.where(valid, out_ref[...], -1.0)
+            if slot:
+                rin[0] = jnp.maximum(rin[0], rin[slot])
+
+    out_ref[...] = jnp.where(valid, rin[0], -1.0).reshape(size)
     for slot in range(SLOTS):
         when(homes_if[slot], lambda slot=slot: result_copy(slot).wait_send())
 
@@ -366,10 +390,12 @@
         vmem = pl.BlockSpec(memory_space=pltpu.VMEM)
         nearest = pl.pallas_call(
             functools.partial(kernel, rows, cols),
-            out_shape=jax.ShapeDtypeStruct((1, size), jnp.float32),
-            in_specs=[vmem, vmem, pl.BlockSpec(memory_space=pltpu.SMEM)],
+            out_shape=jax.ShapeDtypeStruct((size,), jnp.float32),
+            in_specs=[pl.BlockSpec(memory_space=pltpu.HBM), vmem, pl.BlockSpec(memory_space=pltpu.SMEM)],
             out_specs=vmem,
             scratch_shapes=[
+                pltpu.VMEM((size, depth), jnp.bfloat16),
+                pltpu.SemaphoreType.DMA((CHUNKS,)),
                 pltpu.VMEM((size, depth), jnp.bfloat16),
                 pltpu.VMEM((CHUNKS // routes, size // CHUNKS, depth), jnp.bfloat16),
                 pltpu.VMEM((SLOTS, size, depth), jnp.bfloat16),
@@ -397,8 +423,8 @@
             cost_estimate=pl.CostEstimate(
                 flops=10 * size * size * depth, bytes_accessed=4 * size * depth, transcendentals=0
             ),
-        )(embeddings, doc_ids.reshape(1, size), valid_counts)
-        return nearest.reshape(size)
+        )(embeddings, doc_ids, valid_counts)
+        return nearest
 
     in_specs = (P(("row", "col"), None), P(("row", "col")), P(("row", "col")))
     return jax.shard_map(

time: 129 us -> 124 us (0.961)
  the two profiles are of different devices: /device:TPU:32 before, /device:TPU:96 now
where the time goes in v3:
time: 124 us
  Pallas kernels  121 us (98%)
  local copies, waits for them, and re-layouts  2.68 us (2%)
    pallas_call x1, Pallas kernels, local(): pl.pallas_call(functools.partial(kernel, rows, cols), out_shape=jax.Shape...  121 us
    unnamed x5, local copies, waits for them, and re-layouts  2.68 us

profile of v3, /device:TPU:96, one launch (start us, length us, event | category | flops | bytes accessed | tf_op | source)
XLA Modules:
  0.0 124.3 jit_solution(12956667313360464083)
XLA Ops:
  0.7 0.0 copy-start
  0.7 1.4 %copy-done = bf16[768,1024]{1,0:T(8,128)(2,1)S(1)} copy-done((bf16[768,1024]{1,0:T(8,128)(2,1)S(1)}, bf16[768,1024]{1,0:T(8,128)(2,1)}, u32[]{:S(2)}) %copy-start) | copy-done | bytes 1572888
  2.1 0.0 copy-start.1
  2.1 0.7 copy-done.1
  2.7 121.0 %shard_map.37 = f32[768]{0:T(1024)S(1)} custom-call(bf16[768,1024]{1,0:T(8,128)(2,1)S(1)} %copy-done, s32[768]{0:T(1024)S(1)} %copy-done.1, s32[1]{0:T(128)S(6)} %copy.5.count_ref), custom_call_target="tpu_custom_call" | custom-call | flops 6039797760 | bytes 3145728 | tf_op jit(solution)/shard_map/pallas_call | solution.py:391
  123.7 0.6 copy.6
Async XLA Ops:
  0.7 1.4 %copy-start = (bf16[768,1024]{1,0:T(8,128)(2,1)S(1)}, bf16[768,1024]{1,0:T(8,128)(2,1)}, u32[]{:S(2)}) copy-start(bf16[768,1024]{1,0:T(8,128)(2,1)} %emb_hbm.1) | copy-start | bytes 4718596
  2.1 0.7 copy-start.1

commit v4 on v3

--- a/solution.py
+++ b/solution.py
@@ -215,15 +215,6 @@
         pl.when(crossing & (c % routes == last))(lambda: first_copy(c, 3, bsend).start())
         pl.when(crossing & (c % routes != last))(lambda: relay_in(c, own).start())
 
-    for slot in range(SLOTS):
-
-        @functools.partial(when, homes_if[slot])
-        def _(slot=slot):
-            key_copy(slot).wait_recv()
-            for g in range(size // LANES):
-                lanes = slice(g * LANES, (g + 1) * LANES)
-                kcol[slot, lanes, :] = jnp.broadcast_to(kin[slot, :, lanes], (LANES, LANES)).T
-
     for turn in range(CHUNKS // routes):
 
         @pl.when(relay_first)
@@ -319,6 +310,16 @@
 
     third = CHUNKS // STEPS
     go(0, third + 4)
+
+    for slot in range(SLOTS):
+
+        @functools.partial(when, homes_if[slot])
+        def _(slot=slot):
+            key_copy(slot).wait_recv()
+            for g in range(size // LANES):
+                lanes = slice(g * LANES, (g + 1) * LANES)
+                kcol[slot, lanes, :] = jnp.broadcast_to(kin[slot, :, lanes], (LANES, LANES)).T
+
     near(0)
     distant(0)
     compute(0, 0, pairs)

time: 124 us -> 124 us (level)
  the two profiles are of different devices: /device:TPU:96 before, /device:TPU:64 now
where the time goes in v4:
time: 124 us
  Pallas kernels  121 us (98%)
  local copies, waits for them, and re-layouts  2.68 us (2%)
    pallas_call x1, Pallas kernels, local(): pl.pallas_call(functools.partial(kernel, rows, cols), out_shape=jax.Shape...  121 us
    unnamed x5, local copies, waits for them, and re-layouts  2.68 us

profile of v4, /device:TPU:64, one launch (start us, length us, event | category | flops | bytes accessed | tf_op | source)
XLA Modules:
  0.0 124.0 jit_solution(885011122828971998)
XLA Ops:
  0.7 0.0 copy-start
  0.7 1.4 %copy-done = bf16[768,1024]{1,0:T(8,128)(2,1)S(1)} copy-done((bf16[768,1024]{1,0:T(8,128)(2,1)S(1)}, bf16[768,1024]{1,0:T(8,128)(2,1)}, u32[]{:S(2)}) %copy-start) | copy-done | bytes 1572888
  2.1 0.0 copy-start.1
  2.1 0.7 copy-done.1
  2.7 120.6 %shard_map.37 = f32[768]{0:T(1024)S(1)} custom-call(bf16[768,1024]{1,0:T(8,128)(2,1)S(1)} %copy-done, s32[768]{0:T(1024)S(1)} %copy-done.1, s32[1]{0:T(128)S(6)} %copy.5.count_ref), custom_call_target="tpu_custom_call" | custom-call | flops 6039797760 | bytes 3145728 | tf_op jit(solution)/shard_map/pallas_call | solution.py:392
  123.4 0.6 copy.6
Async XLA Ops:
  0.7 1.4 %copy-start = (bf16[768,1024]{1,0:T(8,128)(2,1)S(1)}, bf16[768,1024]{1,0:T(8,128)(2,1)}, u32[]{:S(2)}) copy-start(bf16[768,1024]{1,0:T(8,128)(2,1)} %emb_hbm.1) | copy-start | bytes 4718596
  2.1 0.7 copy-start.1
